TPU v7x, 512 devices: a whole 4x4x16 slice. The times are simulated.
512 devices in a mesh: row: 16 (over z_lo, core), col: 32 (over x, y, z_hi).
Axes of the slice: x: 4, y: 4, z: 16 (z_hi: 2, z_lo: 8; z = z_hi * 8 + z_lo), core: 2. Of those that a mesh axis runs over, the one named last changes fastest.
Arguments:
- features: bfloat16 [128, 512, 128], P('row', 'col'), may hold values from -6 to 6
- cotangent: bfloat16 [128, 512, 128], P('row', 'col'), may hold values from -12 to 12
- w_qkv: bfloat16 [128, 384], replicated, may hold values from -0.5 to 0.5
- w_out: bfloat16 [128, 128], replicated, may hold values from -0.5 to 0.5
- cos_scale: float32 [2], replicated, may hold values from 4 to 16
Outputs:
- grad_features: bfloat16 [128, 512, 128], P('row', 'col')
- grad_w_qkv: float32 [128, 384], replicated
- grad_w_out: float32 [128, 128], replicated
- grad_scale: float32 [2], replicated
All inputs are finite; a program needn't handle non-finite values.
Results may differ from a plain program's by a relative error of at most 0.0085.
Values may be sent and summed in bfloat16 or wider, within the bound.
No kernel may reach another device: no remote copies, remote signals or barrier semaphores. Data moves between devices by JAX's collectives and lax.ppermute only.
A program may use at most 128 MiB of HBM per device.

v0:
```python
import functools

import jax
import jax.numpy as jnp
import numpy as np
from jax import lax
from jax.experimental import pallas as pl
from jax.experimental.pallas import tpu as pltpu
from jax.sharding import PartitionSpec as P

RADIUS = 3
EPSILON = 1e-06
MODEL = 128
HEAD = 64
ROWS, COLS = 8, 16
OWN = ROWS * COLS
QUERIES = 368
KEYS = 640
NEAR = 384
BLOCK = 16
EDGE = 24
SENT = 80
SHARES = 32
LOG2E = 1.4426950408889634
FAR_AWAY = 1e4

F32 = jnp.float32
BF16 = jnp.bfloat16


def side_columns(left, inner):
    if left:
        return -3 if inner else -6
    return 16 if inner else 19


def token_table(core):
    def tile(holder, start, count, lift):
        token = start + np.arange(count)
        return np.stack([8 * holder + token // 16 + lift, token % 16])

    def edge(holder, left, inner, lift):
        token = np.arange(EDGE)
        row = 8 * holder + token // 3 + lift
        return np.stack([row, token % 3 + side_columns(left, inner)])

    other = 1 - core
    lift = -16 if core == 0 else 16
    left = core == 0
    pieces = [
        tile(core, 0, 128, 0),
        tile(other, 80 * core, 48, 0),
        edge(core, left, True, 0),
        edge(other, left, True, 0),
        edge(other, not left, True, 0),
        edge(core, not left, True, 0),
        tile(other, 80 * other, 48, lift),
        edge(other, not left, True, lift),
        edge(other, left, True, lift),
        tile(other, 48 - 16 * core, 48, 0),
        edge(core, left, False, 0),
        edge(other, left, False, 0),
        edge(other, not left, False, 0),
        edge(core, not left, False, 0),
        tile(other, 48 - 16 * other, 48, lift),
        edge(other, not left, False, lift),
        edge(other, left, False, lift),
        np.full((2, 32), FAR_AWAY),
    ]
    return np.concatenate(pieces, axis=1).astype(np.float32)


TABLES = np.stack([token_table(0), token_table(1)])


def vmem(count):
    return [pl.BlockSpec(memory_space=pltpu.VMEM)] * count


def dot_nt(left, right):
    return lax.dot_general(
        left, right, (((1,), (1,)), ((), ())), preferred_element_type=F32
    )


def dot_tn(left, right):
    return lax.dot_general(
        left, right, (((0,), (0,)), ((), ())), preferred_element_type=F32
    )


def dot_nn(left, right):
    return jnp.dot(left, right, preferred_element_type=F32)


def edge_kernel(tile, own_edge, mate_message):
    core, _, _ = place_here()
    spot = lax.broadcasted_iota(jnp.int32, (SENT, 128), 0)
    token = lax.broadcasted_iota(jnp.int32, (SENT, 128), 1)
    kind = jnp.where(spot >= EDGE, 1, 0) + jnp.where(spot >= 2 * EDGE, 1, 0)
    index = spot - EDGE * kind
    row = (index * 43) >> 7
    step = index - 3 * row
    outer = kind == 1
    right = row * 16 + step + jnp.where(outer, 10, 13)
    left = row * 16 + step + jnp.where(outer, 3, 0)
    used = spot < 3 * EDGE
    from_cot = kind == 2
    for ref, wanted in (
        (own_edge, jnp.where(core == 0, right, left)),
        (mate_message, jnp.where(core == 0, left, right)),
    ):
        hit = (wanted == token) & used
        of_feat = jnp.where(hit & ~from_cot, 1.0, 0.0).astype(BF16)
        of_cot = jnp.where(hit & from_cot, 1.0, 0.0).astype(BF16)
        ref[0:SENT, :] = (
            dot_nn(of_feat, tile[0:OWN, :]) + dot_nn(of_cot, tile[OWN:, :])
        ).astype(BF16)
    half = 1 - core
    mate_message[SENT : SENT + 48, :] = rows_at(tile, 80 * half, 48)
    mate_message[SENT + 48 : SENT + 96, :] = rows_at(tile, 48 - 16 * half, 48)
    mate_message[SENT + 96 : SENT + 144, :] = rows_at(tile, OWN + 80 * half, 48)


def place_here():
    row, col = lax.axis_index("row"), lax.axis_index("col")
    return row & 1, (row >> 1) * 16, col * 16


def rows_at(ref, start, count):
    return ref[pl.ds(pl.multiple_of(start, 16), count), :]


def prepare_kernel(tile, _, w_qkv, w_out, key_spots, tile_copy, weights, bias):
    tile_copy[...] = tile[...]
    for part in range(3):
        columns = slice(part * MODEL, (part + 1) * MODEL)
        weights[columns, :] = w_qkv[:, columns]
    weights[3 * MODEL :, :] = w_out[...]

    core, first_row, first_col = place_here()
    spots = jnp.where(core == 0, key_spots[0], key_spots[1])
    key_rows, key_cols = spots[0:1, :], spots[1:2, :]
    turn = lax.broadcasted_iota(jnp.int32, (16, MODEL), 0)
    turn = jnp.where(turn == lax.broadcasted_iota(jnp.int32, (16, MODEL), 1), 1.0, 0.0)
    query_spots = dot_tn(spots[:, :NEAR].astype(BF16), turn.astype(BF16))
    all_rows = key_rows + first_row.astype(F32)
    all_cols = key_cols + first_col.astype(F32)
    inside = (all_rows >= 0) & (all_rows < 128) & (all_cols >= 0) & (all_cols < 512)
    key_rows = jnp.where(inside, key_rows, FAR_AWAY)
    for start in range(0, QUERIES, BLOCK):
        here = query_spots[start : start + BLOCK, :]
        apart = jnp.maximum(
            jnp.abs(here[:, 0:1] - key_rows), jnp.abs(here[:, 1:2] - key_cols)
        )
        bias[start : start + BLOCK, :] = jnp.where(apart <= RADIUS, 0.0, -1e30)


def attention_kernel(
    scales,
    tile,
    weights,
    mate,
    next_chip,
    far,
    far_skip,
    far_next,
    far_mate,
    bias,
    grad_feat,
    grad_w,
    grad_scale,
    tokens,
    cots,
    keys,
    values,
    queries,
    d_attn,
    raw,
    dots,
    mix_own,
    mix_key,
    slope_own,
    slope_key,
):
    core, _, _ = place_here()
    other = 1 - core
    w_query, w_key, w_value, w_out = (
        weights[start : start + MODEL, :] for start in range(0, 4 * MODEL, MODEL)
    )
    far_wide = far[...].astype(F32)
    mate_wide = far_mate[...].astype(F32)
    next_wide = far_next[0:SENT, :].astype(F32)
    skip_wide = far_skip[SENT:, :].astype(F32)
    edges = (
        far_wide[:SENT],
        far_wide[SENT:],
        mate_wide[:SENT],
        mate_wide[SENT:],
        next_wide,
        skip_wide,
    )

    def strip(kind, chosen):
        pieces = [edge[kind * EDGE : (kind + 1) * EDGE] for edge in chosen]
        return jnp.concatenate(pieces, axis=0).astype(BF16)

    tokens[0:128, :] = tile[0:OWN, :]
    tokens[128:176, :] = mate[SENT : SENT + 48, :]
    tokens[176:272, :] = strip(0, edges[:4])
    tokens[272:320, :] = rows_at(next_chip, 80 * other, 48)
    tokens[320:368, :] = strip(0, edges[4:])
    tokens[368:416, :] = mate[SENT + 48 : SENT + 96, :]
    tokens[416:512, :] = strip(1, edges[:4])
    tokens[512:560, :] = rows_at(next_chip, 48 - 16 * other, 48)
    tokens[560:608, :] = strip(1, edges[4:])
    tokens[608:640, :] = jnp.zeros((32, MODEL), BF16)
    cots[0:128, :] = tile[OWN:, :]
    cots[128:176, :] = mate[SENT + 96 : SENT + 144, :]
    cots[176:272, :] = strip(2, edges[:4])
    cots[272:320, :] = rows_at(next_chip, OWN + 80 * other, 48)
    cots[320:368, :] = strip(2, edges[4:])

    keys[...] = dot_nn(tokens[...], w_key).astype(BF16)
    values[...] = dot_nn(tokens[...], w_value).astype(BF16)
    queries[...] = dot_nn(tokens[0:QUERIES, :], w_query).astype(BF16)
    d_attn[...] = dot_nt(cots[...], w_out).astype(BF16)

    key_wide = keys[...].astype(F32)
    square = key_wide * key_wide
    upper = square.astype(BF16)
    lower = (square - upper.astype(F32)).astype(BF16)
    head_of = lax.broadcasted_iota(jnp.int32, (16, MODEL), 1) // HEAD
    picks = jnp.where(
        head_of == lax.broadcasted_iota(jnp.int32, (16, MODEL), 0), 1.0, 0.0
    ).astype(BF16)
    key_inverse = lax.rsqrt(dot_nt(picks, upper) + dot_nt(picks, lower) + EPSILON)

    first = lax.broadcasted_iota(jnp.int32, (1, MODEL), 1) < HEAD

    def head_sums(array):
        low = jnp.sum(jnp.where(first, array, 0.0), axis=1, keepdims=True)
        high = jnp.sum(jnp.where(first, 0.0, array), axis=1, keepdims=True)
        return low, high

    for head in range(2):
        own_lanes = first if head == 0 else ~first
        raw[head] = dot_nt(jnp.where(own_lanes, queries[...], 0.0).astype(BF16), keys[...])
        dots[head] = dot_nt(jnp.where(own_lanes, d_attn[...], 0.0).astype(BF16), values[...])

    key_inv = [key_inverse[head : head + 1, :] for head in range(2)]
    wide = jnp.concatenate([scales[...]] * (KEYS // MODEL), axis=1)
    key_reach = [key_inv[head] * wide[head : head + 1, :] for head in range(2)]
    scale_lanes = jnp.where(first, scales[0:1, :], scales[1:2, :])
    scale_sums = [jnp.zeros((BLOCK, 1), F32), jnp.zeros((BLOCK, 1), F32)]
    for start in range(0, QUERIES, BLOCK):
        rows = slice(start, start + BLOCK)
        width = NEAR if start < OWN else KEYS
        query_wide = queries[rows, :].astype(F32)
        norms = head_sums(query_wide * query_wide)
        for head in range(2):
            inverse = lax.rsqrt(norms[head] + EPSILON)
            score = raw[head, rows, :width] * (inverse * LOG2E) * key_reach[head][:, :width]
            expo = jnp.exp2(score + bias[rows, :width])
            gain = dots[head, rows, :width]
            share = 1.0 / (jnp.sum(expo, axis=1, keepdims=True) + 1e-30)
            center = jnp.sum(expo * gain, axis=1, keepdims=True) * share
            if start < OWN:
                weight = expo[:, :NEAR] * share
                slope = weight * (gain[:, :NEAR] - center)
                pull = slope * key_inv[head][:, :NEAR]
                scale_sums[head] += inverse * jnp.sum(
                    pull * raw[head, rows, :NEAR], axis=1, keepdims=True
                )
                mix_own[head, rows, :] = weight.astype(BF16)
                slope_own[head, rows, :] = pull.astype(BF16)
                weight = weight[:, :OWN]
                slope = slope[:, :OWN]
            else:
                weight = expo[:, :OWN] * share
                slope = weight * (gain[:, :OWN] - center)
            mix_key[head, rows, :] = weight.astype(BF16)
            slope_key[head, rows, :] = (slope * inverse).astype(BF16)

    def both(dot, left, right):
        return jnp.where(first, dot(left[0], right), dot(left[1], right))

    attn_out = both(dot_nn, mix_own, values[0:NEAR, :]).astype(BF16)
    dq_unit = scale_lanes * both(dot_nn, slope_own, keys[0:NEAR, :])
    dk_unit = scale_lanes * both(dot_tn, slope_key, queries[...])
    dv = both(dot_tn, mix_key, d_attn[...])

    def unit_backward(vector, grad_unit):
        low, high = head_sums(vector * vector)
        inverse = jnp.where(first, lax.rsqrt(low + EPSILON), lax.rsqrt(high + EPSILON))
        unit = vector * inverse
        low, high = head_sums(unit * grad_unit)
        return (grad_unit - unit * jnp.where(first, low, high)) * inverse

    dq = unit_backward(queries[0:OWN, :].astype(F32), dq_unit).astype(BF16)
    dk = unit_backward(keys[0:OWN, :].astype(F32), dk_unit).astype(BF16)
    dv = dv.astype(BF16)
    grad_feat[...] = (
        dot_nt(dq, w_query)
        + dot_nt(dk, w_key)
        + dot_nt(dv, w_value)
    ).astype(BF16)
    norm = 1.0 / 256.0
    for part, grad in enumerate((dq, dk, dv)):
        grad_w[part * MODEL : (part + 1) * MODEL, :] = (
            dot_tn(tile[0:OWN, :], grad) * norm
        ).astype(BF16)
    grad_w[3 * MODEL :, :] = (dot_tn(attn_out, tile[OWN:, :]) * norm).astype(BF16)

    lane = lax.broadcasted_iota(jnp.int32, (8, MODEL), 1)
    part = lax.broadcasted_iota(jnp.int32, (8, MODEL), 0)
    terms = [jnp.sum(total, axis=0, keepdims=True) * norm for total in scale_sums]
    rest = jnp.where(part == 0, terms[0], terms[1])
    held = jnp.zeros((8, MODEL), F32)
    for which in range(3):
        piece = rest.astype(BF16).astype(F32)
        held = jnp.where(lane == which, piece, held)
        rest = rest - piece
    grad_scale[...] = held.astype(BF16)


def result_kernel(whole, terms, feat_tile, grad_feat, grad_w_qkv, grad_w_out, grad_scale):
    grad_feat[...] = feat_tile[...]
    for part in range(3):
        rows = slice(part * MODEL, (part + 1) * MODEL)
        grad_w_qkv[:, rows] = whole[rows, :].astype(F32)
    grad_w_out[...] = whole[3 * MODEL :, :].astype(F32)
    for head in range(2):
        grad_scale[head] = jnp.sum(terms[head : head + 1, :])


def pairs(target):
    found = []
    for row in range(16):
        for col in range(32):
            to_row, to_col = target(row, col)
            if 0 <= to_row < 16 and 0 <= to_col < 32:
                found.append((row * 32 + col, to_row * 32 + to_col))
    return found


EVERY = ("row", "col")


def device(x, y, z, core):
    return ((z % 8) * 2 + core) * 32 + (x % 4) * 8 + (y % 4) * 2 + z // 8 % 2


FIRST_X, FIRST_Y, FIRST_Z = 2, 2, 9


def apart(place):
    return min(place[0], 4 - place[0]) + min(place[1], 4 - place[1])


PLACES = sorted(
    ((x, y, core) for x in range(4) for y in range(4) for core in (1, 0)),
    key=lambda place: (place != (0, 0, 1), -apart(place)),
)
PLANES = [
    [device(x + FIRST_X, y + FIRST_Y, z, core) for x, y, core in PLACES] for z in range(16)
]
LINES = [
    [device(x, y, z + FIRST_Z, core) for z in range(16)]
    for x in range(4)
    for y in range(4)
    for core in range(2)
]
CHIP_MATE = pairs(lambda row, col: (row ^ 1, col))
FAR_MATE = pairs(lambda row, col: (row, col - 1 if row % 2 else col + 1))
NEXT_CHIP = pairs(lambda row, col: (row + 1 if row % 2 else row - 1, col))
SKIP_CHIP = pairs(lambda row, col: (row - 2 if row % 2 else row + 2, col))


def exchange(array, groups):
    return lax.all_to_all(array, EVERY, 0, 0, axis_index_groups=groups, tiled=True)


def to_all(array, groups):
    return exchange(jnp.broadcast_to(array[None], (len(groups[0]),) + array.shape), groups)


def on_device(features, cotangent, w_qkv, w_out, cos_scale):
    feat = features.reshape(OWN, MODEL)
    cot = cotangent.reshape(OWN, MODEL)
    smem = pl.BlockSpec(memory_space=pltpu.SMEM)

    edge = jax.ShapeDtypeStruct((SENT, MODEL), BF16)
    tile = jnp.concatenate([feat, cot])
    own_edge, mate_message = pl.pallas_call(
        edge_kernel,
        out_shape=(edge, jax.ShapeDtypeStruct((SENT + 144, MODEL), BF16)),
        in_specs=vmem(1),
        out_specs=vmem(2),
        compiler_params=pltpu.CompilerParams(vmem_limit_bytes=2 * 1024 * 1024),
        name="edges",
    )(tile)
    mate = lax.ppermute(mate_message, EVERY, CHIP_MATE)
    other_edge = mate[:SENT]
    far = lax.ppermute(jnp.concatenate([own_edge, other_edge]), EVERY, FAR_MATE)
    key_spots = np.zeros((2, 16, KEYS), np.float32)
    key_spots[:, :2] = TABLES
    key_spots = jnp.asarray(key_spots)
    scales = jnp.broadcast_to(cos_scale[None, :, None], (4, 2, MODEL)).reshape(8, MODEL)
    tile_copy, weights, bias = pl.pallas_call(
        prepare_kernel,
        out_shape=(
            jax.ShapeDtypeStruct((2 * OWN, MODEL), BF16),
            jax.ShapeDtypeStruct((4 * MODEL, MODEL), BF16),
            jax.ShapeDtypeStruct((QUERIES, KEYS), F32),
        ),
        in_specs=vmem(5),
        out_specs=vmem(3),
        compiler_params=pltpu.CompilerParams(vmem_limit_bytes=4 * 1024 * 1024),
        cost_estimate=pl.CostEstimate(
            flops=1000000, bytes_accessed=1 << 20, transcendentals=0
        ),
        name="prepare",
    )(tile, mate, w_qkv, w_out, key_spots)
    next_chip = lax.ppermute(tile_copy, EVERY, NEXT_CHIP)

    far_mate = lax.ppermute(far, EVERY, CHIP_MATE)
    far_next = lax.ppermute(far, EVERY, NEXT_CHIP)
    far_skip = lax.ppermute(far, EVERY, SKIP_CHIP)
    grad_feat, grad_w, scale_tile = pl.pallas_call(
        attention_kernel,
        out_shape=(
            jax.ShapeDtypeStruct((OWN, MODEL), BF16),
            jax.ShapeDtypeStruct((4 * MODEL, MODEL), BF16),
            jax.ShapeDtypeStruct((8, MODEL), BF16),
        ),
        in_specs=vmem(10),
        out_specs=vmem(3),
        scratch_shapes=[
            pltpu.VMEM((KEYS, MODEL), BF16),
            pltpu.VMEM((QUERIES, MODEL), BF16),
            pltpu.VMEM((KEYS, MODEL), BF16),
            pltpu.VMEM((KEYS, MODEL), BF16),
            pltpu.VMEM((QUERIES, MODEL), BF16),
            pltpu.VMEM((QUERIES, MODEL), BF16),
            pltpu.VMEM((2, QUERIES, KEYS), F32),
            pltpu.VMEM((2, QUERIES, KEYS), F32),
            pltpu.VMEM((2, OWN, NEAR), BF16),
            pltpu.VMEM((2, QUERIES, OWN), BF16),
            pltpu.VMEM((2, OWN, NEAR), BF16),
            pltpu.VMEM((2, QUERIES, OWN), BF16),
        ],
        compiler_params=pltpu.CompilerParams(vmem_limit_bytes=16 * 1024 * 1024),
        name="window_attention",
    )(
        scales,
        tile,
        weights,
        mate,
        next_chip,
        far,
        far_skip,
        far_next,
        far_mate,
        bias,
    )

    scale_rows = jnp.broadcast_to(scale_tile[None, None, :2], (SHARES, 1, 2, MODEL))
    shares = jnp.concatenate([grad_w.reshape(SHARES, 8, 2, MODEL), scale_rows], axis=1)
    lane = lax.broadcasted_iota(jnp.int32, (2, MODEL), 1)
    shares, lane = lax.optimization_barrier((shares, lane))
    share = jnp.sum(exchange(shares, PLANES).astype(F32), axis=0)
    term = jnp.sum(jnp.where(lane < 3, share[8], 0.0), axis=1, keepdims=True)
    top = lax.reduce_precision(term, 8, 7)
    middle = lax.reduce_precision(term - top, 8, 7)
    parts = jnp.where(lane == 0, top, jnp.where(lane == 1, middle, term - top - middle))
    parts = jnp.where(lane < 3, parts, 0.0)
    share = jnp.concatenate([share[:8], parts[None]], axis=0).astype(BF16)
    share = jnp.sum(to_all(share, LINES).astype(F32), axis=0)
    share, terms = lax.optimization_barrier((share[:8].astype(BF16).reshape(16, MODEL), share[8]))
    whole = to_all(share, PLANES).reshape(4 * MODEL, MODEL)
    grad_feat, grad_w_qkv, grad_w_out, grad_scale = pl.pallas_call(
        result_kernel,
        out_shape=(
            jax.ShapeDtypeStruct((OWN, MODEL), BF16),
            jax.ShapeDtypeStruct((MODEL, 3 * MODEL), F32),
            jax.ShapeDtypeStruct((MODEL, MODEL), F32),
            jax.ShapeDtypeStruct((2,), F32),
        ),
        in_specs=vmem(3),
        out_specs=vmem(3) + [smem],
        compiler_params=pltpu.CompilerParams(vmem_limit_bytes=2 * 1024 * 1024),
        name="results",
    )(whole, terms, grad_feat)
    return (grad_feat.reshape(ROWS, COLS, MODEL), grad_w_qkv, grad_w_out, grad_scale)


def solution(mesh):
    tokens = P("row", "col", None)
    return jax.shard_map(
        on_device,
        mesh=mesh,
        in_specs=(tokens, tokens, P(), P(), P()),
        out_specs=(tokens, P(), P(), P()),
        check_vma=False,
    )
```

profile of v0, /device:TPU:1, one launch (start us, length us, event | category | flops | bytes accessed | tf_op | source)
XLA Modules:
  0.0 79.5 jit_solution(5773348239214865363)
XLA Ops:
  0.6 0.0 copy-start.2
  0.6 0.8 pad_maximum_fusion.1.tile
  1.4 0.2 edges.1
  1.6 8.8 %collective-permute-start = (bf16[224,128]{1,0:T(8,128)(2,1)S(1)}, bf16[224,128]{1,0:T(8,128)(2,1)S(1)}, u32[]{:S(2)}, u32[]{:S(2)}) collective-permute-start(bf16[224,128]{1,0:T(8,128)(2,1)S(1)} %get-tuple-element.20), channel_id=1, source_target_pairs={{0,32},{1,33},{2,34},{3,35},{4,36},{5,37},{6,38},{7,39},{8,40},{9,... | collective-permute-start | bytes 172040 | tf_op jit(solution)/shard_map/ppermute | solution.py:403
  10.4 0.9 %collective-permute-done._.mate = bf16[224,128]{1,0:T(8,128)(2,1)S(1)} collective-permute-done((bf16[224,128]{1,0:T(8,128)(2,1)S(1)}, bf16[224,128]{1,0:T(8,128)(2,1)S(1)}, u32[]{:S(2)}, u32[]{:S(2)}) %collective-permute-start) | collective-permute-done | bytes 57376 | tf_op jit(solution)/shard_map/ppermute | solution.py:403
  11.3 1.3 %collective-permute-start.2 = (bf16[160,128]{1,0:T(8,128)(2,1)S(1)}, bf16[160,128]{1,0:T(8,128)(2,1)S(1)}, u32[]{:S(2)}, u32[]{:S(2)}) collective-permute-start(bf16[160,128]{1,0:T(8,128)(2,1)S(1)} %pad_maximum_fusion.2), channel_id=1, source_target_pairs={{0,1},{1,2},{2,3},{3,4},{4,5},{5,6},{6,7},{7,8},{8,9},{9,10},{10,1... | collective-permute-start | bytes 122888 | tf_op jit(solution)/shard_map/ppermute | solution.py:405
  12.6 0.0 copy-done.2
  12.6 0.0 copy-done
  12.6 0.0 copy-done.1
  12.6 0.5 prepare.1
  13.1 0.0 copy-start.3
  13.1 11.9 %collective-permute-start.1 = (bf16[256,128]{1,0:T(8,128)(2,1)S(1)}, bf16[256,128]{1,0:T(8,128)(2,1)S(1)}, u32[]{:S(2)}, u32[]{:S(2)}) collective-permute-start(bf16[256,128]{1,0:T(8,128)(2,1)S(1)} %get-tuple-element.22), channel_id=1, source_target_pairs={{32,64},{33,65},{34,66},{35,67},{36,68},{37,69},{38,70},{39,71},{4... | collective-permute-start | bytes 196616 | tf_op jit(solution)/shard_map/ppermute | solution.py:425
  25.1 0.0 collective-permute-done.2.far
  25.1 1.3 %collective-permute-start.3 = (bf16[160,128]{1,0:T(8,128)(2,1)S(1)}, bf16[160,128]{1,0:T(8,128)(2,1)S(1)}, u32[]{:S(2)}, u32[]{:S(2)}) collective-permute-start(bf16[160,128]{1,0:T(8,128)(2,1)S(1)} %collective-permute-done.2.far), channel_id=1, source_target_pairs={{0,64},{1,65},{2,66},{3,67},{4,68},{5,69},{6,70},{7,71},{8,72},{9,... | collective-permute-start | bytes 122888 | tf_op jit(solution)/shard_map/ppermute | solution.py:429
  26.4 3.6 %collective-permute-start.4 = (bf16[160,128]{1,0:T(8,128)(2,1)S(1)}, bf16[160,128]{1,0:T(8,128)(2,1)S(1)}, u32[]{:S(2)}, u32[]{:S(2)}) collective-permute-start(bf16[160,128]{1,0:T(8,128)(2,1)S(1)} %collective-permute-done.2.far), channel_id=1, source_target_pairs={{32,64},{33,65},{34,66},{35,67},{36,68},{37,69},{38,70},{39,71},{4... | collective-permute-start | bytes 122888 | tf_op jit(solution)/shard_map/ppermute | solution.py:428
  29.9 1.9 %collective-permute-start.5 = (bf16[160,128]{1,0:T(8,128)(2,1)S(1)}, bf16[160,128]{1,0:T(8,128)(2,1)S(1)}, u32[]{:S(2)}, u32[]{:S(2)}) collective-permute-start(bf16[160,128]{1,0:T(8,128)(2,1)S(1)} %collective-permute-done.2.far), channel_id=1, source_target_pairs={{0,32},{1,33},{2,34},{3,35},{4,36},{5,37},{6,38},{7,39},{8,40},{9,... | collective-permute-start | bytes 122888 | tf_op jit(solution)/shard_map/ppermute | solution.py:427
  31.9 0.0 copy-done.3
  31.9 0.1 broadcast_in_dim.60
  32.0 0.0 collective-permute-done.1.next_chip
  32.0 0.0 collective-permute-done.3.far_skip
  32.0 0.0 collective-permute-done.4.far_next
  32.0 1.1 %collective-permute-done.5.far_mate = bf16[160,128]{1,0:T(8,128)(2,1)S(1)} collective-permute-done((bf16[160,128]{1,0:T(8,128)(2,1)S(1)}, bf16[160,128]{1,0:T(8,128)(2,1)S(1)}, u32[]{:S(2)}, u32[]{:S(2)}) %collective-permute-start.5) | collective-permute-done | bytes 40992 | tf_op jit(solution)/shard_map/ppermute | solution.py:427
  33.0 0.1 broadcast_in_dim.61.scales
  33.1 1.8 %window_attention.1 = (bf16[128,128]{1,0:T(8,128)(2,1)S(1)}, bf16[512,128]{1,0:T(8,128)(2,1)S(1)}, bf16[8,128]{1,0:T(8,128)(2,1)S(1)}) custom-call(f32[8,128]{1,0:T(8,128)S(1)} %broadcast_in_dim.61.scales, bf16[256,128]{1,0:T(8,128)(2,1)S(1)} %pad_maximum_fusion.1.tile, bf16[512,128]{1,0:T(8,128)(2,1)S(1)} %get-tuple-element.21.weights, ...), custom_call_target="tpu_custom_call" | custom-call | tf_op jit(solution)/shard_map/window_attention/pallas_call | solution.py:430
  35.0 0.2 pad_maximum_fusion
  35.2 13.5 %all_to_all.15 = bf16[32,9,2,128]{3,2,1,0:T(2,128)(2,1)S(1)} all-to-all(bf16[32,9,2,128]{3,2,1,0:T(2,128)(2,1)S(1)} %pad_maximum_fusion), channel_id=1, replica_groups={{52,32,0,56,24,38,6,34,2,40,8,48,16,62,30,58,26,36,4,46,14,42,10,54,22,..., dimensions={0} | all-to-all | bytes 294912 | tf_op jit(solution)/shard_map/all_to_all | solution.py:381
  48.7 0.1 convert_reduce_fusion
  48.9 0.1 fusion.3
  49.0 0.1 fusion.4
  49.2 18.4 %all_to_all.16 = bf16[16,9,2,128]{3,2,1,0:T(2,128)(2,1)S(1)} all-to-all(bf16[16,9,2,128]{3,2,1,0:T(2,128)(2,1)S(1)} %broadcast_in_dim.67), channel_id=1, replica_groups={{65,129,193,257,321,385,449,0,64,128,192,256,320,384,448,1},{97,161,225..., dimensions={0} | all-to-all | bytes 147456 | tf_op jit(solution)/shard_map/all_to_all | solution.py:381
  67.7 11.1 %all_to_all.17 = bf16[32,16,128]{2,1,0:T(8,128)(2,1)S(1)} all-to-all(bf16[32,16,128]{2,1,0:T(8,128)(2,1)S(1)} %broadcast_in_dim.68), channel_id=1, replica_groups={{52,32,0,56,24,38,6,34,2,40,8,48,16,62,30,58,26,36,4,46,14,42,10,54,22,..., dimensions={0} | all-to-all | bytes 262144 | tf_op jit(solution)/shard_map/all_to_all | solution.py:381
  78.8 0.7 results.1
  (16 shorter events, 0.2 us)
Async XLA Ops:
  0.6 11.9 %copy-start.2 = (bf16[128,128]{1,0:T(8,128)(2,1)S(1)}, bf16[128,128]{1,0:T(8,128)(2,1)}, u32[]{:S(2)}) copy-start(bf16[128,128]{1,0:T(8,128)(2,1)} %w_out.1) | copy-start | bytes 98308
  1.4 11.2 %copy-start = (bf16[128,384]{1,0:T(8,128)(2,1)S(1)}, bf16[128,384]{1,0:T(8,128)(2,1)}, u32[]{:S(2)}) copy-start(bf16[128,384]{1,0:T(8,128)(2,1)} %w_qkv.1) | copy-start | bytes 294916
  1.4 11.2 %copy-start.1 = (f32[2,16,640]{2,1,0:T(8,128)S(1)}, f32[2,16,640]{2,1,0:T(8,128)}, u32[]{:S(2)}) copy-start(f32[2,16,640]{2,1,0:T(8,128)} %constant.10.clone.key_spots) | copy-start | bytes 245764
  1.6 9.7 %collective-permute-start = (bf16[224,128]{1,0:T(8,128)(2,1)S(1)}, bf16[224,128]{1,0:T(8,128)(2,1)S(1)}, u32[]{:S(2)}, u32[]{:S(2)}) collective-permute-start(bf16[224,128]{1,0:T(8,128)(2,1)S(1)} %get-tuple-element.20), channel_id=1, source_target_pairs={{0,32},{1,33},{2,34},{3,35},{4,36},{5,37},{6,38},{7,39},{8,40},{9,... | collective-permute-start | bytes 172040 | tf_op jit(solution)/shard_map/ppermute | solution.py:403
  11.3 13.8 %collective-permute-start.2 = (bf16[160,128]{1,0:T(8,128)(2,1)S(1)}, bf16[160,128]{1,0:T(8,128)(2,1)S(1)}, u32[]{:S(2)}, u32[]{:S(2)}) collective-permute-start(bf16[160,128]{1,0:T(8,128)(2,1)S(1)} %pad_maximum_fusion.2), channel_id=1, source_target_pairs={{0,1},{1,2},{2,3},{3,4},{4,5},{5,6},{6,7},{7,8},{8,9},{9,10},{10,1... | collective-permute-start | bytes 122888 | tf_op jit(solution)/shard_map/ppermute | solution.py:405
  13.1 18.8 %copy-start.3 = (f32[2]{0:T(128)S(1)}, f32[2]{0:T(128)}, u32[]{:S(2)}) copy-start(f32[2]{0:T(128)} %param.10) | copy-start | bytes 28
  13.1 18.9 %collective-permute-start.1 = (bf16[256,128]{1,0:T(8,128)(2,1)S(1)}, bf16[256,128]{1,0:T(8,128)(2,1)S(1)}, u32[]{:S(2)}, u32[]{:S(2)}) collective-permute-start(bf16[256,128]{1,0:T(8,128)(2,1)S(1)} %get-tuple-element.22), channel_id=1, source_target_pairs={{32,64},{33,65},{34,66},{35,67},{36,68},{37,69},{38,70},{39,71},{4... | collective-permute-start | bytes 196616 | tf_op jit(solution)/shard_map/ppermute | solution.py:425
  25.1 6.9 %collective-permute-start.3 = (bf16[160,128]{1,0:T(8,128)(2,1)S(1)}, bf16[160,128]{1,0:T(8,128)(2,1)S(1)}, u32[]{:S(2)}, u32[]{:S(2)}) collective-permute-start(bf16[160,128]{1,0:T(8,128)(2,1)S(1)} %collective-permute-done.2.far), channel_id=1, source_target_pairs={{0,64},{1,65},{2,66},{3,67},{4,68},{5,69},{6,70},{7,71},{8,72},{9,... | collective-permute-start | bytes 122888 | tf_op jit(solution)/shard_map/ppermute | solution.py:429
  26.4 5.6 %collective-permute-start.4 = (bf16[160,128]{1,0:T(8,128)(2,1)S(1)}, bf16[160,128]{1,0:T(8,128)(2,1)S(1)}, u32[]{:S(2)}, u32[]{:S(2)}) collective-permute-start(bf16[160,128]{1,0:T(8,128)(2,1)S(1)} %collective-permute-done.2.far), channel_id=1, source_target_pairs={{32,64},{33,65},{34,66},{35,67},{36,68},{37,69},{38,70},{39,71},{4... | collective-permute-start | bytes 122888 | tf_op jit(solution)/shard_map/ppermute | solution.py:428
  29.9 3.1 %collective-permute-start.5 = (bf16[160,128]{1,0:T(8,128)(2,1)S(1)}, bf16[160,128]{1,0:T(8,128)(2,1)S(1)}, u32[]{:S(2)}, u32[]{:S(2)}) collective-permute-start(bf16[160,128]{1,0:T(8,128)(2,1)S(1)} %collective-permute-done.2.far), channel_id=1, source_target_pairs={{0,32},{1,33},{2,34},{3,35},{4,36},{5,37},{6,38},{7,39},{8,40},{9,... | collective-permute-start | bytes 122888 | tf_op jit(solution)/shard_map/ppermute | solution.py:427
where the time goes:
time: 79.9 us; the launch traced here: 79.5 us
  blocking collectives  43 us (54%)
  starting transfers between devices  28.8 us (36%)
  Pallas kernels  3.23 us (4%)
  waiting for transfers between devices  1.95 us (2%)
  other arithmetic  1.38 us (2%)
  between operations  0.84 us (1%)
    all_to_all x3, blocking collectives, exchange(): lax.all_to_all(array, EVERY, 0, 0, axis_index_groups=groups, tiled=True)  43 us
    ppermute x1, starting transfers between devices, on_device(): next_chip = lax.ppermute(tile_copy, EVERY, NEXT_CHIP)  11.9 us
    ppermute x1, starting transfers between devices, on_device(): mate = lax.ppermute(mate_message, EVERY, CHIP_MATE)  8.79 us
    ppermute x1, starting transfers between devices, on_device(): far_next = lax.ppermute(far, EVERY, NEXT_CHIP)  3.56 us
    ppermute x1, starting transfers between devices, on_device(): far_mate = lax.ppermute(far, EVERY, CHIP_MATE)  1.92 us
    pallas_call x1, Pallas kernels, on_device(): pl.pallas_call(attention_kernel, out_shape=(jax.ShapeDtypeStruct((OWN, MO...  1.85 us
  transfers between devices with their start and end apart: 6, of which 2 were waited for; matrix products, arithmetic and copies ran while one was open for 0% of the time, Pallas kernels for 1%

commit v1 on v0

--- a/solution.py
+++ b/solution.py
@@ -221,8 +221,9 @@
     cots[272:320, :] = rows_at(next_chip, OWN + 80 * other, 48)
     cots[320:368, :] = strip(2, edges[4:])
 
-    keys[...] = dot_nn(tokens[...], w_key).astype(BF16)
-    values[...] = dot_nn(tokens[...], w_value).astype(BF16)
+    both_kinds = dot_nn(tokens[...], jnp.concatenate([w_key, w_value], axis=1)).astype(BF16)
+    keys[...] = both_kinds[:, :MODEL]
+    values[...] = both_kinds[:, MODEL:]
     queries[...] = dot_nn(tokens[0:QUERIES, :], w_query).astype(BF16)
     d_attn[...] = dot_nt(cots[...], w_out).astype(BF16)
 
@@ -245,8 +246,11 @@
 
     for head in range(2):
         own_lanes = first if head == 0 else ~first
-        raw[head] = dot_nt(jnp.where(own_lanes, queries[...], 0.0).astype(BF16), keys[...])
-        dots[head] = dot_nt(jnp.where(own_lanes, d_attn[...], 0.0).astype(BF16), values[...])
+        for rows, width in ((slice(0, OWN), NEAR), (slice(OWN, QUERIES), KEYS)):
+            query = jnp.where(own_lanes, queries[rows, :], 0.0).astype(BF16)
+            grad = jnp.where(own_lanes, d_attn[rows, :], 0.0).astype(BF16)
+            raw[head, rows, :width] = dot_nt(query, keys[0:width, :])
+            dots[head, rows, :width] = dot_nt(grad, values[0:width, :])
 
     key_inv = [key_inverse[head : head + 1, :] for head in range(2)]
     wide = jnp.concatenate([scales[...]] * (KEYS // MODEL), axis=1)

time: 79.9 us -> 80 us (level)
  no operation moved by 1% of the time
where the time goes in v1:
time: 80 us; the launch traced here: 79.5 us
  blocking collectives  43 us (54%)
  starting transfers between devices  28.8 us (36%)
  Pallas kernels  3.27 us (4%)
  waiting for transfers between devices  1.95 us (2%)
  other arithmetic  1.38 us (2%)
  between operations  0.85 us (1%)
    all_to_all x3, blocking collectives, exchange(): lax.all_to_all(array, EVERY, 0, 0, axis_index_groups=groups, tiled=True)  43 us
    ppermute x1, starting transfers between devices, on_device(): next_chip = lax.ppermute(tile_copy, EVERY, NEXT_CHIP)  11.9 us
    ppermute x1, starting transfers between devices, on_device(): mate = lax.ppermute(mate_message, EVERY, CHIP_MATE)  8.79 us
    ppermute x1, starting transfers between devices, on_device(): far_next = lax.ppermute(far, EVERY, NEXT_CHIP)  3.56 us
    ppermute x1, starting transfers between devices, on_device(): far_mate = lax.ppermute(far, EVERY, CHIP_MATE)  1.92 us
    pallas_call x1, Pallas kernels, on_device(): pl.pallas_call(attention_kernel, out_shape=(jax.ShapeDtypeStruct((OWN, MO...  1.88 us
  transfers between devices with their start and end apart: 6, of which 2 were waited for; matrix products, arithmetic and copies ran while one was open for 0% of the time, Pallas kernels for 1%

profile of v1, /device:TPU:1, one launch (start us, length us, event | category | flops | bytes accessed | tf_op | source)
XLA Modules:
  0.0 79.5 jit_solution(15642654616343863089)
XLA Ops:
  0.6 0.0 copy-start.2
  0.6 0.8 pad_maximum_fusion.1.tile
  1.4 0.2 edges.1
  1.6 8.8 %collective-permute-start = (bf16[224,128]{1,0:T(8,128)(2,1)S(1)}, bf16[224,128]{1,0:T(8,128)(2,1)S(1)}, u32[]{:S(2)}, u32[]{:S(2)}) collective-permute-start(bf16[224,128]{1,0:T(8,128)(2,1)S(1)} %get-tuple-element.20), channel_id=1, source_target_pairs={{0,32},{1,33},{2,34},{3,35},{4,36},{5,37},{6,38},{7,39},{8,40},{9,... | collective-permute-start | bytes 172040 | tf_op jit(solution)/shard_map/ppermute | solution.py:407
  10.4 0.9 %collective-permute-done._.mate = bf16[224,128]{1,0:T(8,128)(2,1)S(1)} collective-permute-done((bf16[224,128]{1,0:T(8,128)(2,1)S(1)}, bf16[224,128]{1,0:T(8,128)(2,1)S(1)}, u32[]{:S(2)}, u32[]{:S(2)}) %collective-permute-start) | collective-permute-done | bytes 57376 | tf_op jit(solution)/shard_map/ppermute | solution.py:407
  11.3 1.3 %collective-permute-start.2 = (bf16[160,128]{1,0:T(8,128)(2,1)S(1)}, bf16[160,128]{1,0:T(8,128)(2,1)S(1)}, u32[]{:S(2)}, u32[]{:S(2)}) collective-permute-start(bf16[160,128]{1,0:T(8,128)(2,1)S(1)} %pad_maximum_fusion.2), channel_id=1, source_target_pairs={{0,1},{1,2},{2,3},{3,4},{4,5},{5,6},{6,7},{7,8},{8,9},{9,10},{10,1... | collective-permute-start | bytes 122888 | tf_op jit(solution)/shard_map/ppermute | solution.py:409
  12.6 0.0 copy-done.2
  12.6 0.0 copy-done
  12.6 0.0 copy-done.1
  12.6 0.5 prepare.1
  13.1 0.0 copy-start.3
  13.1 11.9 %collective-permute-start.1 = (bf16[256,128]{1,0:T(8,128)(2,1)S(1)}, bf16[256,128]{1,0:T(8,128)(2,1)S(1)}, u32[]{:S(2)}, u32[]{:S(2)}) collective-permute-start(bf16[256,128]{1,0:T(8,128)(2,1)S(1)} %get-tuple-element.22), channel_id=1, source_target_pairs={{32,64},{33,65},{34,66},{35,67},{36,68},{37,69},{38,70},{39,71},{4... | collective-permute-start | bytes 196616 | tf_op jit(solution)/shard_map/ppermute | solution.py:429
  25.1 0.0 collective-permute-done.2.far
  25.1 1.3 %collective-permute-start.3 = (bf16[160,128]{1,0:T(8,128)(2,1)S(1)}, bf16[160,128]{1,0:T(8,128)(2,1)S(1)}, u32[]{:S(2)}, u32[]{:S(2)}) collective-permute-start(bf16[160,128]{1,0:T(8,128)(2,1)S(1)} %collective-permute-done.2.far), channel_id=1, source_target_pairs={{0,64},{1,65},{2,66},{3,67},{4,68},{5,69},{6,70},{7,71},{8,72},{9,... | collective-permute-start | bytes 122888 | tf_op jit(solution)/shard_map/ppermute | solution.py:433
  26.4 3.6 %collective-permute-start.4 = (bf16[160,128]{1,0:T(8,128)(2,1)S(1)}, bf16[160,128]{1,0:T(8,128)(2,1)S(1)}, u32[]{:S(2)}, u32[]{:S(2)}) collective-permute-start(bf16[160,128]{1,0:T(8,128)(2,1)S(1)} %collective-permute-done.2.far), channel_id=1, source_target_pairs={{32,64},{33,65},{34,66},{35,67},{36,68},{37,69},{38,70},{39,71},{4... | collective-permute-start | bytes 122888 | tf_op jit(solution)/shard_map/ppermute | solution.py:432
  29.9 1.9 %collective-permute-start.5 = (bf16[160,128]{1,0:T(8,128)(2,1)S(1)}, bf16[160,128]{1,0:T(8,128)(2,1)S(1)}, u32[]{:S(2)}, u32[]{:S(2)}) collective-permute-start(bf16[160,128]{1,0:T(8,128)(2,1)S(1)} %collective-permute-done.2.far), channel_id=1, source_target_pairs={{0,32},{1,33},{2,34},{3,35},{4,36},{5,37},{6,38},{7,39},{8,40},{9,... | collective-permute-start | bytes 122888 | tf_op jit(solution)/shard_map/ppermute | solution.py:431
  31.9 0.0 copy-done.3
  31.9 0.1 broadcast_in_dim.60
  32.0 0.0 collective-permute-done.1.next_chip
  32.0 0.0 collective-permute-done.3.far_skip
  32.0 0.0 collective-permute-done.4.far_next
  32.0 1.1 %collective-permute-done.5.far_mate = bf16[160,128]{1,0:T(8,128)(2,1)S(1)} collective-permute-done((bf16[160,128]{1,0:T(8,128)(2,1)S(1)}, bf16[160,128]{1,0:T(8,128)(2,1)S(1)}, u32[]{:S(2)}, u32[]{:S(2)}) %collective-permute-start.5) | collective-permute-done | bytes 40992 | tf_op jit(solution)/shard_map/ppermute | solution.py:431
  33.0 0.1 broadcast_in_dim.61.scales
  33.1 1.9 %window_attention.1 = (bf16[128,128]{1,0:T(8,128)(2,1)S(1)}, bf16[512,128]{1,0:T(8,128)(2,1)S(1)}, bf16[8,128]{1,0:T(8,128)(2,1)S(1)}) custom-call(f32[8,128]{1,0:T(8,128)S(1)} %broadcast_in_dim.61.scales, bf16[256,128]{1,0:T(8,128)(2,1)S(1)} %pad_maximum_fusion.1.tile, bf16[512,128]{1,0:T(8,128)(2,1)S(1)} %get-tuple-element.21.weights, ...), custom_call_target="tpu_custom_call" | custom-call | tf_op jit(solution)/shard_map/window_attention/pallas_call | solution.py:434
  35.0 0.2 pad_maximum_fusion
  35.3 13.5 %all_to_all.15 = bf16[32,9,2,128]{3,2,1,0:T(2,128)(2,1)S(1)} all-to-all(bf16[32,9,2,128]{3,2,1,0:T(2,128)(2,1)S(1)} %pad_maximum_fusion), channel_id=1, replica_groups={{52,32,0,56,24,38,6,34,2,40,8,48,16,62,30,58,26,36,4,46,14,42,10,54,22,..., dimensions={0} | all-to-all | bytes 294912 | tf_op jit(solution)/shard_map/all_to_all | solution.py:385
  48.8 0.1 convert_reduce_fusion
  48.9 0.1 fusion.3
  49.1 0.1 fusion.4
  49.2 18.4 %all_to_all.16 = bf16[16,9,2,128]{3,2,1,0:T(2,128)(2,1)S(1)} all-to-all(bf16[16,9,2,128]{3,2,1,0:T(2,128)(2,1)S(1)} %broadcast_in_dim.67), channel_id=1, replica_groups={{65,129,193,257,321,385,449,0,64,128,192,256,320,384,448,1},{97,161,225..., dimensions={0} | all-to-all | bytes 147456 | tf_op jit(solution)/shard_map/all_to_all | solution.py:385
  67.7 11.1 %all_to_all.17 = bf16[32,16,128]{2,1,0:T(8,128)(2,1)S(1)} all-to-all(bf16[32,16,128]{2,1,0:T(8,128)(2,1)S(1)} %broadcast_in_dim.68), channel_id=1, replica_groups={{52,32,0,56,24,38,6,34,2,40,8,48,16,62,30,58,26,36,4,46,14,42,10,54,22,..., dimensions={0} | all-to-all | bytes 262144 | tf_op jit(solution)/shard_map/all_to_all | solution.py:385
  78.8 0.7 results.1
  (16 shorter events, 0.2 us)
Async XLA Ops:
  0.6 11.9 %copy-start.2 = (bf16[128,128]{1,0:T(8,128)(2,1)S(1)}, bf16[128,128]{1,0:T(8,128)(2,1)}, u32[]{:S(2)}) copy-start(bf16[128,128]{1,0:T(8,128)(2,1)} %w_out.1) | copy-start | bytes 98308
  1.4 11.2 %copy-start = (bf16[128,384]{1,0:T(8,128)(2,1)S(1)}, bf16[128,384]{1,0:T(8,128)(2,1)}, u32[]{:S(2)}) copy-start(bf16[128,384]{1,0:T(8,128)(2,1)} %w_qkv.1) | copy-start | bytes 294916
  1.4 11.2 %copy-start.1 = (f32[2,16,640]{2,1,0:T(8,128)S(1)}, f32[2,16,640]{2,1,0:T(8,128)}, u32[]{:S(2)}) copy-start(f32[2,16,640]{2,1,0:T(8,128)} %constant.10.clone.key_spots) | copy-start | bytes 245764
  1.6 9.7 %collective-permute-start = (bf16[224,128]{1,0:T(8,128)(2,1)S(1)}, bf16[224,128]{1,0:T(8,128)(2,1)S(1)}, u32[]{:S(2)}, u32[]{:S(2)}) collective-permute-start(bf16[224,128]{1,0:T(8,128)(2,1)S(1)} %get-tuple-element.20), channel_id=1, source_target_pairs={{0,32},{1,33},{2,34},{3,35},{4,36},{5,37},{6,38},{7,39},{8,40},{9,... | collective-permute-start | bytes 172040 | tf_op jit(solution)/shard_map/ppermute | solution.py:407
  11.3 13.8 %collective-permute-start.2 = (bf16[160,128]{1,0:T(8,128)(2,1)S(1)}, bf16[160,128]{1,0:T(8,128)(2,1)S(1)}, u32[]{:S(2)}, u32[]{:S(2)}) collective-permute-start(bf16[160,128]{1,0:T(8,128)(2,1)S(1)} %pad_maximum_fusion.2), channel_id=1, source_target_pairs={{0,1},{1,2},{2,3},{3,4},{4,5},{5,6},{6,7},{7,8},{8,9},{9,10},{10,1... | collective-permute-start | bytes 122888 | tf_op jit(solution)/shard_map/ppermute | solution.py:409
  13.1 18.8 %copy-start.3 = (f32[2]{0:T(128)S(1)}, f32[2]{0:T(128)}, u32[]{:S(2)}) copy-start(f32[2]{0:T(128)} %param.10) | copy-start | bytes 28
  13.1 18.9 %collective-permute-start.1 = (bf16[256,128]{1,0:T(8,128)(2,1)S(1)}, bf16[256,128]{1,0:T(8,128)(2,1)S(1)}, u32[]{:S(2)}, u32[]{:S(2)}) collective-permute-start(bf16[256,128]{1,0:T(8,128)(2,1)S(1)} %get-tuple-element.22), channel_id=1, source_target_pairs={{32,64},{33,65},{34,66},{35,67},{36,68},{37,69},{38,70},{39,71},{4... | collective-permute-start | bytes 196616 | tf_op jit(solution)/shard_map/ppermute | solution.py:429
  25.1 6.9 %collective-permute-start.3 = (bf16[160,128]{1,0:T(8,128)(2,1)S(1)}, bf16[160,128]{1,0:T(8,128)(2,1)S(1)}, u32[]{:S(2)}, u32[]{:S(2)}) collective-permute-start(bf16[160,128]{1,0:T(8,128)(2,1)S(1)} %collective-permute-done.2.far), channel_id=1, source_target_pairs={{0,64},{1,65},{2,66},{3,67},{4,68},{5,69},{6,70},{7,71},{8,72},{9,... | collective-permute-start | bytes 122888 | tf_op jit(solution)/shard_map/ppermute | solution.py:433
  26.4 5.6 %collective-permute-start.4 = (bf16[160,128]{1,0:T(8,128)(2,1)S(1)}, bf16[160,128]{1,0:T(8,128)(2,1)S(1)}, u32[]{:S(2)}, u32[]{:S(2)}) collective-permute-start(bf16[160,128]{1,0:T(8,128)(2,1)S(1)} %collective-permute-done.2.far), channel_id=1, source_target_pairs={{32,64},{33,65},{34,66},{35,67},{36,68},{37,69},{38,70},{39,71},{4... | collective-permute-start | bytes 122888 | tf_op jit(solution)/shard_map/ppermute | solution.py:432
  29.9 3.1 %collective-permute-start.5 = (bf16[160,128]{1,0:T(8,128)(2,1)S(1)}, bf16[160,128]{1,0:T(8,128)(2,1)S(1)}, u32[]{:S(2)}, u32[]{:S(2)}) collective-permute-start(bf16[160,128]{1,0:T(8,128)(2,1)S(1)} %collective-permute-done.2.far), channel_id=1, source_target_pairs={{0,32},{1,33},{2,34},{3,35},{4,36},{5,37},{6,38},{7,39},{8,40},{9,... | collective-permute-start | bytes 122888 | tf_op jit(solution)/shard_map/ppermute | solution.py:431

commit v2 on v1

--- a/solution.py
+++ b/solution.py
@@ -131,12 +131,19 @@
     return ref[pl.ds(pl.multiple_of(start, 16), count), :]
 
 
-def prepare_kernel(tile, _, w_qkv, w_out, key_spots, tile_copy, weights, bias):
+def prepare_kernel(
+    tile, mate, w_qkv, w_out, key_spots, tile_copy, weights, bias, near_kv, near_q, near_d
+):
     tile_copy[...] = tile[...]
     for part in range(3):
         columns = slice(part * MODEL, (part + 1) * MODEL)
         weights[columns, :] = w_qkv[:, columns]
     weights[3 * MODEL :, :] = w_out[...]
+    near = jnp.concatenate([tile[0:OWN, :], mate[SENT : SENT + 96, :]], axis=0)
+    near_kv[...] = dot_nn(near, w_qkv[:, MODEL:]).astype(BF16)
+    near_q[...] = dot_nn(near[:176], w_qkv[:, :MODEL]).astype(BF16)
+    near_cots = jnp.concatenate([tile[OWN:, :], mate[SENT + 96 : SENT + 144, :]], axis=0)
+    near_d[...] = dot_nt(near_cots, w_out[...]).astype(BF16)
 
     core, first_row, first_col = place_here()
     spots = jnp.where(core == 0, key_spots[0], key_spots[1])
@@ -160,7 +167,9 @@
     scales,
     tile,
     weights,
-    mate,
+    near_kv,
+    near_q,
+    near_d,
     next_chip,
     far,
     far_skip,
@@ -205,27 +214,30 @@
         pieces = [edge[kind * EDGE : (kind + 1) * EDGE] for edge in chosen]
         return jnp.concatenate(pieces, axis=0).astype(BF16)
 
-    tokens[0:128, :] = tile[0:OWN, :]
-    tokens[128:176, :] = mate[SENT : SENT + 48, :]
     tokens[176:272, :] = strip(0, edges[:4])
     tokens[272:320, :] = rows_at(next_chip, 80 * other, 48)
     tokens[320:368, :] = strip(0, edges[4:])
-    tokens[368:416, :] = mate[SENT + 48 : SENT + 96, :]
     tokens[416:512, :] = strip(1, edges[:4])
     tokens[512:560, :] = rows_at(next_chip, 48 - 16 * other, 48)
     tokens[560:608, :] = strip(1, edges[4:])
     tokens[608:640, :] = jnp.zeros((32, MODEL), BF16)
-    cots[0:128, :] = tile[OWN:, :]
-    cots[128:176, :] = mate[SENT + 96 : SENT + 144, :]
     cots[176:272, :] = strip(2, edges[:4])
     cots[272:320, :] = rows_at(next_chip, OWN + 80 * other, 48)
     cots[320:368, :] = strip(2, edges[4:])
 
-    both_kinds = dot_nn(tokens[...], jnp.concatenate([w_key, w_value], axis=1)).astype(BF16)
-    keys[...] = both_kinds[:, :MODEL]
-    values[...] = both_kinds[:, MODEL:]
-    queries[...] = dot_nn(tokens[0:QUERIES, :], w_query).astype(BF16)
-    d_attn[...] = dot_nt(cots[...], w_out).astype(BF16)
+    w_both = jnp.concatenate([w_key, w_value], axis=1)
+    for rows, projected in (
+        (slice(0, 176), near_kv[0:176, :]),
+        (slice(368, 416), near_kv[176:224, :]),
+        (slice(176, 368), dot_nn(tokens[176:368, :], w_both).astype(BF16)),
+        (slice(416, KEYS), dot_nn(tokens[416:KEYS, :], w_both).astype(BF16)),
+    ):
+        keys[rows, :] = projected[:, :MODEL]
+        values[rows, :] = projected[:, MODEL:]
+    queries[0:176, :] = near_q[...]
+    queries[176:QUERIES, :] = dot_nn(tokens[176:QUERIES, :], w_query).astype(BF16)
+    d_attn[0:176, :] = near_d[...]
+    d_attn[176:QUERIES, :] = dot_nt(cots[176:QUERIES, :], w_out).astype(BF16)
 
     key_wide = keys[...].astype(F32)
     square = key_wide * key_wide
@@ -411,15 +423,18 @@
     key_spots[:, :2] = TABLES
     key_spots = jnp.asarray(key_spots)
     scales = jnp.broadcast_to(cos_scale[None, :, None], (4, 2, MODEL)).reshape(8, MODEL)
-    tile_copy, weights, bias = pl.pallas_call(
+    tile_copy, weights, bias, near_kv, near_q, near_d = pl.pallas_call(
         prepare_kernel,
         out_shape=(
             jax.ShapeDtypeStruct((2 * OWN, MODEL), BF16),
             jax.ShapeDtypeStruct((4 * MODEL, MODEL), BF16),
             jax.ShapeDtypeStruct((QUERIES, KEYS), F32),
+            jax.ShapeDtypeStruct((224, 2 * MODEL), BF16),
+            jax.ShapeDtypeStruct((176, MODEL), BF16),
+            jax.ShapeDtypeStruct((176, MODEL), BF16),
         ),
         in_specs=vmem(5),
-        out_specs=vmem(3),
+        out_specs=vmem(6),
         compiler_params=pltpu.CompilerParams(vmem_limit_bytes=4 * 1024 * 1024),
         cost_estimate=pl.CostEstimate(
             flops=1000000, bytes_accessed=1 << 20, transcendentals=0
@@ -438,7 +453,7 @@
             jax.ShapeDtypeStruct((4 * MODEL, MODEL), BF16),
             jax.ShapeDtypeStruct((8, MODEL), BF16),
         ),
-        in_specs=vmem(10),
+        in_specs=vmem(12),
         out_specs=vmem(3),
         scratch_shapes=[
             pltpu.VMEM((KEYS, MODEL), BF16),
@@ -460,7 +475,9 @@
         scales,
         tile,
         weights,
-        mate,
+        near_kv,
+        near_q,
+        near_d,
         next_chip,
         far,
         far_skip,

time: 80 us -> 79.9 us (level)
  no operation moved by 1% of the time
where the time goes in v2:
time: 79.9 us; the launch traced here: 79.5 us
  blocking collectives  43 us (54%)
  starting transfers between devices  28.8 us (36%)
  Pallas kernels  3.22 us (4%)
  waiting for transfers between devices  1.95 us (2%)
  other arithmetic  1.38 us (2%)
  between operations  0.85 us (1%)
    all_to_all x3, blocking collectives, exchange(): lax.all_to_all(array, EVERY, 0, 0, axis_index_groups=groups, tiled=True)  43 us
    ppermute x1, starting transfers between devices, on_device(): next_chip = lax.ppermute(tile_copy, EVERY, NEXT_CHIP)  11.9 us
    ppermute x1, starting transfers between devices, on_device(): mate = lax.ppermute(mate_message, EVERY, CHIP_MATE)  8.79 us
    ppermute x1, starting transfers between devices, on_device(): far_next = lax.ppermute(far, EVERY, NEXT_CHIP)  3.56 us
    ppermute x1, starting transfers between devices, on_device(): far_mate = lax.ppermute(far, EVERY, CHIP_MATE)  1.92 us
    pallas_call x1, Pallas kernels, on_device(): pl.pallas_call(attention_kernel, out_shape=(jax.ShapeDtypeStruct((OWN, MO...  1.81 us
  transfers between devices with their start and end apart: 6, of which 2 were waited for; matrix products, arithmetic and copies ran while one was open for 0% of the time, Pallas kernels for 1%

profile of v2, /device:TPU:1, one launch (start us, length us, event | category | flops | bytes accessed | tf_op | source)
XLA Modules:
  0.0 79.5 jit_solution(17158233910841801205)
XLA Ops:
  0.6 0.0 copy-start.2
  0.6 0.8 pad_maximum_fusion.1.tile
  1.4 0.2 edges.1
  1.6 8.8 %collective-permute-start = (bf16[224,128]{1,0:T(8,128)(2,1)S(1)}, bf16[224,128]{1,0:T(8,128)(2,1)S(1)}, u32[]{:S(2)}, u32[]{:S(2)}) collective-permute-start(bf16[224,128]{1,0:T(8,128)(2,1)S(1)} %get-tuple-element.23), channel_id=1, source_target_pairs={{0,32},{1,33},{2,34},{3,35},{4,36},{5,37},{6,38},{7,39},{8,40},{9,... | collective-permute-start | bytes 172040 | tf_op jit(solution)/shard_map/ppermute | solution.py:419
  10.4 0.9 %collective-permute-done.mate = bf16[224,128]{1,0:T(8,128)(2,1)S(1)} collective-permute-done((bf16[224,128]{1,0:T(8,128)(2,1)S(1)}, bf16[224,128]{1,0:T(8,128)(2,1)S(1)}, u32[]{:S(2)}, u32[]{:S(2)}) %collective-permute-start) | collective-permute-done | bytes 57376 | tf_op jit(solution)/shard_map/ppermute | solution.py:419
  11.3 1.3 %collective-permute-start.2 = (bf16[160,128]{1,0:T(8,128)(2,1)S(1)}, bf16[160,128]{1,0:T(8,128)(2,1)S(1)}, u32[]{:S(2)}, u32[]{:S(2)}) collective-permute-start(bf16[160,128]{1,0:T(8,128)(2,1)S(1)} %pad_maximum_fusion.2), channel_id=1, source_target_pairs={{0,1},{1,2},{2,3},{3,4},{4,5},{5,6},{6,7},{7,8},{8,9},{9,10},{10,1... | collective-permute-start | bytes 122888 | tf_op jit(solution)/shard_map/ppermute | solution.py:421
  12.6 0.0 copy-done.2
  12.6 0.0 copy-done
  12.6 0.0 copy-done.1
  12.6 0.5 prepare.1
  13.1 0.0 copy-start.3
  13.1 11.9 %collective-permute-start.1 = (bf16[256,128]{1,0:T(8,128)(2,1)S(1)}, bf16[256,128]{1,0:T(8,128)(2,1)S(1)}, u32[]{:S(2)}, u32[]{:S(2)}) collective-permute-start(bf16[256,128]{1,0:T(8,128)(2,1)S(1)} %get-tuple-element.28), channel_id=1, source_target_pairs={{32,64},{33,65},{34,66},{35,67},{36,68},{37,69},{38,70},{39,71},{4... | collective-permute-start | bytes 196616 | tf_op jit(solution)/shard_map/ppermute | solution.py:444
  25.1 0.0 collective-permute-done.2.far
  25.1 1.3 %collective-permute-start.3 = (bf16[160,128]{1,0:T(8,128)(2,1)S(1)}, bf16[160,128]{1,0:T(8,128)(2,1)S(1)}, u32[]{:S(2)}, u32[]{:S(2)}) collective-permute-start(bf16[160,128]{1,0:T(8,128)(2,1)S(1)} %collective-permute-done.2.far), channel_id=1, source_target_pairs={{0,64},{1,65},{2,66},{3,67},{4,68},{5,69},{6,70},{7,71},{8,72},{9,... | collective-permute-start | bytes 122888 | tf_op jit(solution)/shard_map/ppermute | solution.py:448
  26.4 3.6 %collective-permute-start.4 = (bf16[160,128]{1,0:T(8,128)(2,1)S(1)}, bf16[160,128]{1,0:T(8,128)(2,1)S(1)}, u32[]{:S(2)}, u32[]{:S(2)}) collective-permute-start(bf16[160,128]{1,0:T(8,128)(2,1)S(1)} %collective-permute-done.2.far), channel_id=1, source_target_pairs={{32,64},{33,65},{34,66},{35,67},{36,68},{37,69},{38,70},{39,71},{4... | collective-permute-start | bytes 122888 | tf_op jit(solution)/shard_map/ppermute | solution.py:447
  30.0 1.9 %collective-permute-start.5 = (bf16[160,128]{1,0:T(8,128)(2,1)S(1)}, bf16[160,128]{1,0:T(8,128)(2,1)S(1)}, u32[]{:S(2)}, u32[]{:S(2)}) collective-permute-start(bf16[160,128]{1,0:T(8,128)(2,1)S(1)} %collective-permute-done.2.far), channel_id=1, source_target_pairs={{0,32},{1,33},{2,34},{3,35},{4,36},{5,37},{6,38},{7,39},{8,40},{9,... | collective-permute-start | bytes 122888 | tf_op jit(solution)/shard_map/ppermute | solution.py:446
  31.9 0.0 copy-done.3
  31.9 0.1 broadcast_in_dim.60
  32.0 0.0 collective-permute-done.1.next_chip
  32.0 0.0 collective-permute-done.3.far_skip
  32.0 0.0 collective-permute-done.4.far_next
  32.0 1.1 %collective-permute-done.5.far_mate = bf16[160,128]{1,0:T(8,128)(2,1)S(1)} collective-permute-done((bf16[160,128]{1,0:T(8,128)(2,1)S(1)}, bf16[160,128]{1,0:T(8,128)(2,1)S(1)}, u32[]{:S(2)}, u32[]{:S(2)}) %collective-permute-start.5) | collective-permute-done | bytes 40992 | tf_op jit(solution)/shard_map/ppermute | solution.py:446
  33.1 0.1 broadcast_in_dim.61.scales
  33.1 1.8 %window_attention.1 = (bf16[128,128]{1,0:T(8,128)(2,1)S(1)}, bf16[512,128]{1,0:T(8,128)(2,1)S(1)}, bf16[8,128]{1,0:T(8,128)(2,1)S(1)}) custom-call(f32[8,128]{1,0:T(8,128)S(1)} %broadcast_in_dim.61.scales, bf16[256,128]{1,0:T(8,128)(2,1)S(1)} %pad_maximum_fusion.1.tile, bf16[512,128]{1,0:T(8,128)(2,1)S(1)} %get-tuple-element.24.weights, ...), custom_call_target="tpu_custom_call" | custom-call | tf_op jit(solution)/shard_map/window_attention/pallas_call | solution.py:449
  35.0 0.2 pad_maximum_fusion
  35.2 13.5 %all_to_all.15 = bf16[32,9,2,128]{3,2,1,0:T(2,128)(2,1)S(1)} all-to-all(bf16[32,9,2,128]{3,2,1,0:T(2,128)(2,1)S(1)} %pad_maximum_fusion), channel_id=1, replica_groups={{52,32,0,56,24,38,6,34,2,40,8,48,16,62,30,58,26,36,4,46,14,42,10,54,22,..., dimensions={0} | all-to-all | bytes 294912 | tf_op jit(solution)/shard_map/all_to_all | solution.py:397
  48.7 0.1 convert_reduce_fusion
  48.9 0.1 fusion.3
  49.0 0.1 fusion.4
  49.2 18.4 %all_to_all.16 = bf16[16,9,2,128]{3,2,1,0:T(2,128)(2,1)S(1)} all-to-all(bf16[16,9,2,128]{3,2,1,0:T(2,128)(2,1)S(1)} %broadcast_in_dim.67), channel_id=1, replica_groups={{65,129,193,257,321,385,449,0,64,128,192,256,320,384,448,1},{97,161,225..., dimensions={0} | all-to-all | bytes 147456 | tf_op jit(solution)/shard_map/all_to_all | solution.py:397
  67.7 11.1 %all_to_all.17 = bf16[32,16,128]{2,1,0:T(8,128)(2,1)S(1)} all-to-all(bf16[32,16,128]{2,1,0:T(8,128)(2,1)S(1)} %broadcast_in_dim.68), channel_id=1, replica_groups={{52,32,0,56,24,38,6,34,2,40,8,48,16,62,30,58,26,36,4,46,14,42,10,54,22,..., dimensions={0} | all-to-all | bytes 262144 | tf_op jit(solution)/shard_map/all_to_all | solution.py:397
  78.7 0.7 results.1
  (16 shorter events, 0.2 us)
Async XLA Ops:
  0.6 11.9 %copy-start.2 = (bf16[128,128]{1,0:T(8,128)(2,1)S(1)}, bf16[128,128]{1,0:T(8,128)(2,1)}, u32[]{:S(2)}) copy-start(bf16[128,128]{1,0:T(8,128)(2,1)} %w_out.1) | copy-start | bytes 98308
  1.4 11.2 %copy-start = (bf16[128,384]{1,0:T(8,128)(2,1)S(1)}, bf16[128,384]{1,0:T(8,128)(2,1)}, u32[]{:S(2)}) copy-start(bf16[128,384]{1,0:T(8,128)(2,1)} %w_qkv.1) | copy-start | bytes 294916
  1.4 11.2 %copy-start.1 = (f32[2,16,640]{2,1,0:T(8,128)S(1)}, f32[2,16,640]{2,1,0:T(8,128)}, u32[]{:S(2)}) copy-start(f32[2,16,640]{2,1,0:T(8,128)} %constant.10.clone.key_spots) | copy-start | bytes 245764
  1.6 9.7 %collective-permute-start = (bf16[224,128]{1,0:T(8,128)(2,1)S(1)}, bf16[224,128]{1,0:T(8,128)(2,1)S(1)}, u32[]{:S(2)}, u32[]{:S(2)}) collective-permute-start(bf16[224,128]{1,0:T(8,128)(2,1)S(1)} %get-tuple-element.23), channel_id=1, source_target_pairs={{0,32},{1,33},{2,34},{3,35},{4,36},{5,37},{6,38},{7,39},{8,40},{9,... | collective-permute-start | bytes 172040 | tf_op jit(solution)/shard_map/ppermute | solution.py:419
  11.3 13.8 %collective-permute-start.2 = (bf16[160,128]{1,0:T(8,128)(2,1)S(1)}, bf16[160,128]{1,0:T(8,128)(2,1)S(1)}, u32[]{:S(2)}, u32[]{:S(2)}) collective-permute-start(bf16[160,128]{1,0:T(8,128)(2,1)S(1)} %pad_maximum_fusion.2), channel_id=1, source_target_pairs={{0,1},{1,2},{2,3},{3,4},{4,5},{5,6},{6,7},{7,8},{8,9},{9,10},{10,1... | collective-permute-start | bytes 122888 | tf_op jit(solution)/shard_map/ppermute | solution.py:421
  13.1 18.8 %copy-start.3 = (f32[2]{0:T(128)S(1)}, f32[2]{0:T(128)}, u32[]{:S(2)}) copy-start(f32[2]{0:T(128)} %param.10) | copy-start | bytes 28
  13.1 18.9 %collective-permute-start.1 = (bf16[256,128]{1,0:T(8,128)(2,1)S(1)}, bf16[256,128]{1,0:T(8,128)(2,1)S(1)}, u32[]{:S(2)}, u32[]{:S(2)}) collective-permute-start(bf16[256,128]{1,0:T(8,128)(2,1)S(1)} %get-tuple-element.28), channel_id=1, source_target_pairs={{32,64},{33,65},{34,66},{35,67},{36,68},{37,69},{38,70},{39,71},{4... | collective-permute-start | bytes 196616 | tf_op jit(solution)/shard_map/ppermute | solution.py:444
  25.1 6.9 %collective-permute-start.3 = (bf16[160,128]{1,0:T(8,128)(2,1)S(1)}, bf16[160,128]{1,0:T(8,128)(2,1)S(1)}, u32[]{:S(2)}, u32[]{:S(2)}) collective-permute-start(bf16[160,128]{1,0:T(8,128)(2,1)S(1)} %collective-permute-done.2.far), channel_id=1, source_target_pairs={{0,64},{1,65},{2,66},{3,67},{4,68},{5,69},{6,70},{7,71},{8,72},{9,... | collective-permute-start | bytes 122888 | tf_op jit(solution)/shard_map/ppermute | solution.py:448
  26.4 5.6 %collective-permute-start.4 = (bf16[160,128]{1,0:T(8,128)(2,1)S(1)}, bf16[160,128]{1,0:T(8,128)(2,1)S(1)}, u32[]{:S(2)}, u32[]{:S(2)}) collective-permute-start(bf16[160,128]{1,0:T(8,128)(2,1)S(1)} %collective-permute-done.2.far), channel_id=1, source_target_pairs={{32,64},{33,65},{34,66},{35,67},{36,68},{37,69},{38,70},{39,71},{4... | collective-permute-start | bytes 122888 | tf_op jit(solution)/shard_map/ppermute | solution.py:447
  30.0 3.1 %collective-permute-start.5 = (bf16[160,128]{1,0:T(8,128)(2,1)S(1)}, bf16[160,128]{1,0:T(8,128)(2,1)S(1)}, u32[]{:S(2)}, u32[]{:S(2)}) collective-permute-start(bf16[160,128]{1,0:T(8,128)(2,1)S(1)} %collective-permute-done.2.far), channel_id=1, source_target_pairs={{0,32},{1,33},{2,34},{3,35},{4,36},{5,37},{6,38},{7,39},{8,40},{9,... | collective-permute-start | bytes 122888 | tf_op jit(solution)/shard_map/ppermute | solution.py:446

commit v3 on v2

--- a/solution.py
+++ b/solution.py
@@ -382,7 +382,7 @@
     [device(x + FIRST_X, y + FIRST_Y, z, core) for x, y, core in PLACES] for z in range(16)
 ]
 LINES = [
-    [device(x, y, z + FIRST_Z, core) for z in range(16)]
+    [device(x, y, z + FIRST_Z - core, core) for z in range(16)]
     for x in range(4)
     for y in range(4)
     for core in range(2)

time: 79.9 us -> 79.9 us (level)
  no operation moved by 1% of the time
where the time goes in v3:
time: 79.9 us; the launch traced here: 79.5 us
  blocking collectives  43 us (54%)
  starting transfers between devices  28.8 us (36%)
  Pallas kernels  3.22 us (4%)
  waiting for transfers between devices  1.95 us (2%)
  other arithmetic  1.38 us (2%)
  between operations  0.85 us (1%)
    all_to_all x3, blocking collectives, exchange(): lax.all_to_all(array, EVERY, 0, 0, axis_index_groups=groups, tiled=True)  43 us
    ppermute x1, starting transfers between devices, on_device(): next_chip = lax.ppermute(tile_copy, EVERY, NEXT_CHIP)  11.9 us
    ppermute x1, starting transfers between devices, on_device(): mate = lax.ppermute(mate_message, EVERY, CHIP_MATE)  8.79 us
    ppermute x1, starting transfers between devices, on_device(): far_next = lax.ppermute(far, EVERY, NEXT_CHIP)  3.56 us
    ppermute x1, starting transfers between devices, on_device(): far_mate = lax.ppermute(far, EVERY, CHIP_MATE)  1.92 us
    pallas_call x1, Pallas kernels, on_device(): pl.pallas_call(attention_kernel, out_shape=(jax.ShapeDtypeStruct((OWN, MO...  1.81 us
  transfers between devices with their start and end apart: 6, of which 2 were waited for; matrix products, arithmetic and copies ran while one was open for 0% of the time, Pallas kernels for 1%

profile of v3, /device:TPU:1, one launch (start us, length us, event | category | flops | bytes accessed | tf_op | source)
XLA Modules:
  0.0 79.5 jit_solution(5203799542612378988)
XLA Ops:
  0.6 0.0 copy-start.2
  0.6 0.8 pad_maximum_fusion.1.tile
  1.4 0.2 edges.1
  1.6 8.8 %collective-permute-start = (bf16[224,128]{1,0:T(8,128)(2,1)S(1)}, bf16[224,128]{1,0:T(8,128)(2,1)S(1)}, u32[]{:S(2)}, u32[]{:S(2)}) collective-permute-start(bf16[224,128]{1,0:T(8,128)(2,1)S(1)} %get-tuple-element.23), channel_id=1, source_target_pairs={{0,32},{1,33},{2,34},{3,35},{4,36},{5,37},{6,38},{7,39},{8,40},{9,... | collective-permute-start | bytes 172040 | tf_op jit(solution)/shard_map/ppermute | solution.py:419
  10.4 0.9 %collective-permute-done.mate = bf16[224,128]{1,0:T(8,128)(2,1)S(1)} collective-permute-done((bf16[224,128]{1,0:T(8,128)(2,1)S(1)}, bf16[224,128]{1,0:T(8,128)(2,1)S(1)}, u32[]{:S(2)}, u32[]{:S(2)}) %collective-permute-start) | collective-permute-done | bytes 57376 | tf_op jit(solution)/shard_map/ppermute | solution.py:419
  11.3 1.3 %collective-permute-start.2 = (bf16[160,128]{1,0:T(8,128)(2,1)S(1)}, bf16[160,128]{1,0:T(8,128)(2,1)S(1)}, u32[]{:S(2)}, u32[]{:S(2)}) collective-permute-start(bf16[160,128]{1,0:T(8,128)(2,1)S(1)} %pad_maximum_fusion.2), channel_id=1, source_target_pairs={{0,1},{1,2},{2,3},{3,4},{4,5},{5,6},{6,7},{7,8},{8,9},{9,10},{10,1... | collective-permute-start | bytes 122888 | tf_op jit(solution)/shard_map/ppermute | solution.py:421
  12.6 0.0 copy-done.2
  12.6 0.0 copy-done
  12.6 0.0 copy-done.1
  12.6 0.5 prepare.1
  13.1 0.0 copy-start.3
  13.1 11.9 %collective-permute-start.1 = (bf16[256,128]{1,0:T(8,128)(2,1)S(1)}, bf16[256,128]{1,0:T(8,128)(2,1)S(1)}, u32[]{:S(2)}, u32[]{:S(2)}) collective-permute-start(bf16[256,128]{1,0:T(8,128)(2,1)S(1)} %get-tuple-element.28), channel_id=1, source_target_pairs={{32,64},{33,65},{34,66},{35,67},{36,68},{37,69},{38,70},{39,71},{4... | collective-permute-start | bytes 196616 | tf_op jit(solution)/shard_map/ppermute | solution.py:444
  25.1 0.0 collective-permute-done.2.far
  25.1 1.3 %collective-permute-start.3 = (bf16[160,128]{1,0:T(8,128)(2,1)S(1)}, bf16[160,128]{1,0:T(8,128)(2,1)S(1)}, u32[]{:S(2)}, u32[]{:S(2)}) collective-permute-start(bf16[160,128]{1,0:T(8,128)(2,1)S(1)} %collective-permute-done.2.far), channel_id=1, source_target_pairs={{0,64},{1,65},{2,66},{3,67},{4,68},{5,69},{6,70},{7,71},{8,72},{9,... | collective-permute-start | bytes 122888 | tf_op jit(solution)/shard_map/ppermute | solution.py:448
  26.4 3.6 %collective-permute-start.4 = (bf16[160,128]{1,0:T(8,128)(2,1)S(1)}, bf16[160,128]{1,0:T(8,128)(2,1)S(1)}, u32[]{:S(2)}, u32[]{:S(2)}) collective-permute-start(bf16[160,128]{1,0:T(8,128)(2,1)S(1)} %collective-permute-done.2.far), channel_id=1, source_target_pairs={{32,64},{33,65},{34,66},{35,67},{36,68},{37,69},{38,70},{39,71},{4... | collective-permute-start | bytes 122888 | tf_op jit(solution)/shard_map/ppermute | solution.py:447
  30.0 1.9 %collective-permute-start.5 = (bf16[160,128]{1,0:T(8,128)(2,1)S(1)}, bf16[160,128]{1,0:T(8,128)(2,1)S(1)}, u32[]{:S(2)}, u32[]{:S(2)}) collective-permute-start(bf16[160,128]{1,0:T(8,128)(2,1)S(1)} %collective-permute-done.2.far), channel_id=1, source_target_pairs={{0,32},{1,33},{2,34},{3,35},{4,36},{5,37},{6,38},{7,39},{8,40},{9,... | collective-permute-start | bytes 122888 | tf_op jit(solution)/shard_map/ppermute | solution.py:446
  31.9 0.0 copy-done.3
  31.9 0.1 broadcast_in_dim.60
  32.0 0.0 collective-permute-done.1.next_chip
  32.0 0.0 collective-permute-done.3.far_skip
  32.0 0.0 collective-permute-done.4.far_next
  32.0 1.1 %collective-permute-done.5.far_mate = bf16[160,128]{1,0:T(8,128)(2,1)S(1)} collective-permute-done((bf16[160,128]{1,0:T(8,128)(2,1)S(1)}, bf16[160,128]{1,0:T(8,128)(2,1)S(1)}, u32[]{:S(2)}, u32[]{:S(2)}) %collective-permute-start.5) | collective-permute-done | bytes 40992 | tf_op jit(solution)/shard_map/ppermute | solution.py:446
  33.1 0.1 broadcast_in_dim.61.scales
  33.1 1.8 %window_attention.1 = (bf16[128,128]{1,0:T(8,128)(2,1)S(1)}, bf16[512,128]{1,0:T(8,128)(2,1)S(1)}, bf16[8,128]{1,0:T(8,128)(2,1)S(1)}) custom-call(f32[8,128]{1,0:T(8,128)S(1)} %broadcast_in_dim.61.scales, bf16[256,128]{1,0:T(8,128)(2,1)S(1)} %pad_maximum_fusion.1.tile, bf16[512,128]{1,0:T(8,128)(2,1)S(1)} %get-tuple-element.24.weights, ...), custom_call_target="tpu_custom_call" | custom-call | tf_op jit(solution)/shard_map/window_attention/pallas_call | solution.py:449
  35.0 0.2 pad_maximum_fusion
  35.2 13.5 %all_to_all.15 = bf16[32,9,2,128]{3,2,1,0:T(2,128)(2,1)S(1)} all-to-all(bf16[32,9,2,128]{3,2,1,0:T(2,128)(2,1)S(1)} %pad_maximum_fusion), channel_id=1, replica_groups={{52,32,0,56,24,38,6,34,2,40,8,48,16,62,30,58,26,36,4,46,14,42,10,54,22,..., dimensions={0} | all-to-all | bytes 294912 | tf_op jit(solution)/shard_map/all_to_all | solution.py:397
  48.7 0.1 convert_reduce_fusion
  48.9 0.1 fusion.3
  49.0 0.1 fusion.4
  49.2 19.1 %all_to_all.16 = bf16[16,9,2,128]{3,2,1,0:T(2,128)(2,1)S(1)} all-to-all(bf16[16,9,2,128]{3,2,1,0:T(2,128)(2,1)S(1)} %broadcast_in_dim.67), channel_id=1, replica_groups={{65,129,193,257,321,385,449,0,64,128,192,256,320,384,448,1},{33,97,161,..., dimensions={0} | all-to-all | bytes 147456 | tf_op jit(solution)/shard_map/all_to_all | solution.py:397
  68.4 10.4 %all_to_all.17 = bf16[32,16,128]{2,1,0:T(8,128)(2,1)S(1)} all-to-all(bf16[32,16,128]{2,1,0:T(8,128)(2,1)S(1)} %broadcast_in_dim.68), channel_id=1, replica_groups={{52,32,0,56,24,38,6,34,2,40,8,48,16,62,30,58,26,36,4,46,14,42,10,54,22,..., dimensions={0} | all-to-all | bytes 262144 | tf_op jit(solution)/shard_map/all_to_all | solution.py:397
  78.7 0.7 results.1
  (16 shorter events, 0.2 us)
Async XLA Ops:
  0.6 11.9 %copy-start.2 = (bf16[128,128]{1,0:T(8,128)(2,1)S(1)}, bf16[128,128]{1,0:T(8,128)(2,1)}, u32[]{:S(2)}) copy-start(bf16[128,128]{1,0:T(8,128)(2,1)} %w_out.1) | copy-start | bytes 98308
  1.4 11.2 %copy-start = (bf16[128,384]{1,0:T(8,128)(2,1)S(1)}, bf16[128,384]{1,0:T(8,128)(2,1)}, u32[]{:S(2)}) copy-start(bf16[128,384]{1,0:T(8,128)(2,1)} %w_qkv.1) | copy-start | bytes 294916
  1.4 11.2 %copy-start.1 = (f32[2,16,640]{2,1,0:T(8,128)S(1)}, f32[2,16,640]{2,1,0:T(8,128)}, u32[]{:S(2)}) copy-start(f32[2,16,640]{2,1,0:T(8,128)} %constant.10.clone.key_spots) | copy-start | bytes 245764
  1.6 9.7 %collective-permute-start = (bf16[224,128]{1,0:T(8,128)(2,1)S(1)}, bf16[224,128]{1,0:T(8,128)(2,1)S(1)}, u32[]{:S(2)}, u32[]{:S(2)}) collective-permute-start(bf16[224,128]{1,0:T(8,128)(2,1)S(1)} %get-tuple-element.23), channel_id=1, source_target_pairs={{0,32},{1,33},{2,34},{3,35},{4,36},{5,37},{6,38},{7,39},{8,40},{9,... | collective-permute-start | bytes 172040 | tf_op jit(solution)/shard_map/ppermute | solution.py:419
  11.3 13.8 %collective-permute-start.2 = (bf16[160,128]{1,0:T(8,128)(2,1)S(1)}, bf16[160,128]{1,0:T(8,128)(2,1)S(1)}, u32[]{:S(2)}, u32[]{:S(2)}) collective-permute-start(bf16[160,128]{1,0:T(8,128)(2,1)S(1)} %pad_maximum_fusion.2), channel_id=1, source_target_pairs={{0,1},{1,2},{2,3},{3,4},{4,5},{5,6},{6,7},{7,8},{8,9},{9,10},{10,1... | collective-permute-start | bytes 122888 | tf_op jit(solution)/shard_map/ppermute | solution.py:421
  13.1 18.8 %copy-start.3 = (f32[2]{0:T(128)S(1)}, f32[2]{0:T(128)}, u32[]{:S(2)}) copy-start(f32[2]{0:T(128)} %param.10) | copy-start | bytes 28
  13.1 18.9 %collective-permute-start.1 = (bf16[256,128]{1,0:T(8,128)(2,1)S(1)}, bf16[256,128]{1,0:T(8,128)(2,1)S(1)}, u32[]{:S(2)}, u32[]{:S(2)}) collective-permute-start(bf16[256,128]{1,0:T(8,128)(2,1)S(1)} %get-tuple-element.28), channel_id=1, source_target_pairs={{32,64},{33,65},{34,66},{35,67},{36,68},{37,69},{38,70},{39,71},{4... | collective-permute-start | bytes 196616 | tf_op jit(solution)/shard_map/ppermute | solution.py:444
  25.1 6.9 %collective-permute-start.3 = (bf16[160,128]{1,0:T(8,128)(2,1)S(1)}, bf16[160,128]{1,0:T(8,128)(2,1)S(1)}, u32[]{:S(2)}, u32[]{:S(2)}) collective-permute-start(bf16[160,128]{1,0:T(8,128)(2,1)S(1)} %collective-permute-done.2.far), channel_id=1, source_target_pairs={{0,64},{1,65},{2,66},{3,67},{4,68},{5,69},{6,70},{7,71},{8,72},{9,... | collective-permute-start | bytes 122888 | tf_op jit(solution)/shard_map/ppermute | solution.py:448
  26.4 5.6 %collective-permute-start.4 = (bf16[160,128]{1,0:T(8,128)(2,1)S(1)}, bf16[160,128]{1,0:T(8,128)(2,1)S(1)}, u32[]{:S(2)}, u32[]{:S(2)}) collective-permute-start(bf16[160,128]{1,0:T(8,128)(2,1)S(1)} %collective-permute-done.2.far), channel_id=1, source_target_pairs={{32,64},{33,65},{34,66},{35,67},{36,68},{37,69},{38,70},{39,71},{4... | collective-permute-start | bytes 122888 | tf_op jit(solution)/shard_map/ppermute | solution.py:447
  30.0 3.1 %collective-permute-start.5 = (bf16[160,128]{1,0:T(8,128)(2,1)S(1)}, bf16[160,128]{1,0:T(8,128)(2,1)S(1)}, u32[]{:S(2)}, u32[]{:S(2)}) collective-permute-start(bf16[160,128]{1,0:T(8,128)(2,1)S(1)} %collective-permute-done.2.far), channel_id=1, source_target_pairs={{0,32},{1,33},{2,34},{3,35},{4,36},{5,37},{6,38},{7,39},{8,40},{9,... | collective-permute-start | bytes 122888 | tf_op jit(solution)/shard_map/ppermute | solution.py:446
